TPU v7x, 128 devices: a whole 4x4x4 slice. The times are simulated.
128 devices in a mesh: node: 16 (over y, z), local: 8 (over x, core).
Axes of the slice: x: 4, y: 4, z: 4, core: 2. Of those that a mesh axis runs over, the one named last changes fastest.
Arguments:
- tokens: bfloat16 [512, 7168], P(('node', 'local')), may hold values from -6 to 6
- expert_ids: int32 [512, 8], P(('node', 'local')), may hold values from 0 to 31, all different within a row; in each aligned block of 4 rows (0 to 3, 4 to 7, ...) at most 3 rows name the same one
- route_weights: float32 [512, 8], P(('node', 'local')), may hold values from 0.1 to 0.6
- w_gate: bfloat16 [32, 7168, 2048], P('node', None, 'local'), may hold values from -0.0625 to 0.0625
- w_up: bfloat16 [32, 7168, 2048], P('node', None, 'local'), may hold values from -0.0625 to 0.0625
- w_down: bfloat16 [32, 2048, 7168], P('node', 'local'), may hold values from -0.125 to 0.125
Outputs:
- mixed: bfloat16 [512, 7168], P(('node', 'local'))
Inputs may be any that keep to these rules, and one draw needn't show every extreme that they name: `expert_ids`: each row names 8 different experts. Among the rows of one device no expert is named by more than 3 rows, and in every draw some expert is named by exactly 3 rows of some device.
All inputs are finite; a program needn't handle non-finite values.
Results may differ from a plain program's by a relative error of at most 0.0049.
Values may be sent and summed in bfloat16 or wider, within the bound.
A program may use at most 192 MiB of HBM per device.

v0:
```python
import jax
import jax.numpy as jnp
from jax import lax
from jax.sharding import PartitionSpec as P

CAP = 3


def on_device(tokens, expert_ids, route_weights, w_gate, w_up, w_down):
    tok_rows, feat_width = tokens.shape
    per_node = w_gate.shape[0]
    node_count = lax.axis_size("node")
    local_count = lax.axis_size("local")
    expert_count = per_node * node_count
    top_count = expert_ids.shape[1]
    capacity = CAP
    columns = jnp.arange(expert_count, dtype=jnp.int32)
    flat_ids = expert_ids.reshape(-1)
    onehot = (flat_ids[:, None] == columns[None, :]).astype(jnp.int32)
    earlier = jnp.cumsum(onehot, axis=0) - onehot
    slot_index = jnp.sum(earlier * onehot, axis=1)
    home_node = flat_ids // per_node
    inner_slot = flat_ids % per_node
    slot_place = (home_node * capacity + slot_index) * per_node + inner_slot
    n_slots = node_count * capacity * per_node
    places = jnp.arange(n_slots, dtype=jnp.int32)
    matches = (slot_place[:, None] == places[None, :]).reshape(tok_rows, top_count, n_slots)
    selector = jnp.any(matches, axis=1).astype(jnp.bfloat16)
    combine = jnp.sum(jnp.where(matches, route_weights[:, :, None], 0.0), axis=1)
    outgoing = jnp.dot(selector.T, tokens, preferred_element_type=jnp.float32).astype(jnp.bfloat16)
    outgoing = outgoing.reshape(node_count, capacity, per_node, feat_width)
    copies = jnp.broadcast_to(
        outgoing[:, None], (node_count, local_count, capacity, per_node, feat_width)
    )
    copies = copies.reshape(node_count * local_count, capacity, per_node, feat_width)
    arrived = lax.all_to_all(copies, ("node", "local"), split_axis=0, concat_axis=1, tiled=True)
    arrived = arrived.reshape(node_count * local_count * capacity, per_node, feat_width)
    gate_act = jnp.einsum("red,edf->ref", arrived, w_gate, preferred_element_type=jnp.float32)
    up_act = jnp.einsum("red,edf->ref", arrived, w_up, preferred_element_type=jnp.float32)
    partial_value = jnp.einsum(
        "ref,efd->red",
        (jax.nn.silu(gate_act) * up_act).astype(jnp.bfloat16),
        w_down,
        preferred_element_type=jnp.float32,
    )
    partial_value = partial_value.reshape(node_count * local_count, capacity, per_node, feat_width)
    returned = lax.all_to_all(
        partial_value, ("node", "local"), split_axis=0, concat_axis=0, tiled=True
    )
    returned = returned.reshape(node_count, local_count, capacity, per_node, feat_width)
    result = jnp.sum(returned, axis=1)
    mixed = jnp.dot(
        combine,
        result.reshape(n_slots, feat_width),
        precision=lax.Precision.HIGHEST,
        preferred_element_type=jnp.float32,
    )
    return mixed.astype(jnp.bfloat16)


def solution(mesh):
    placed = (
        P(("node", "local"), None),
        P(("node", "local"), None),
        P(("node", "local"), None),
        P("node", None, "local"),
        P("node", None, "local"),
        P("node", "local", None),
    )
    return jax.shard_map(
        on_device, mesh=mesh, in_specs=placed, out_specs=P(("node", "local"), None), check_vma=False
    )
```

profile of v0, /device:TPU:10, one launch (start us, length us, event | category | flops | bytes accessed | tf_op | source)
XLA Modules:
  0.0 565.1 jit_solution(7480824058389388292)
XLA Ops:
  0.0 0.0 copy-start
  0.0 0.8 eq.31
  0.8 0.1 fusion.17
  0.8 0.1 reduce_window_sum.11
  0.9 0.2 select_reduce_fusion.1
  1.1 0.1 reduce_sum.30
  1.2 0.7 fusion.21
  1.9 0.1 fusion.16
  2.0 0.0 copy-done
  2.0 0.6 convolution_convert_fusion
  2.6 0.6 broadcast_in_dim.25
  3.1 6.2 %broadcast_in_dim.26 = bf16[16,8,3,2,7168]{4,3,2,1,0:T(2,128)(2,1)S(1)} broadcast(bf16[16,3,2,7168]{3,2,1,0:T(2,128)(2,1)S(1)} %broadcast_in_dim.25), dimensions={0,2,3,4} | broadcast | bytes 12386304 | tf_op jit(solution)/shard_map/broadcast_in_dim | solution.py:32
  9.3 136.3 %all_to_all.14 = bf16[128,3,2,7168]{3,2,1,0:T(2,128)(2,1)S(1)} all-to-all(bf16[128,3,2,7168]{3,2,1,0:T(2,128)(2,1)S(1)} %bitcast.24), channel_id=1, replica_groups=mesh['node'=16,'local'=8] {'node','local'}, dimensions={0} | all-to-all | bytes 22020096 | tf_op jit(solution)/shard_map/all_to_all | solution.py:36
  145.6 6.6 %fusion.4 = f32[384,2,256]{2,0,1:T(8,128)S(1)} fusion(bf16[2,7168,256]{2,1,0:T(8,128)(2,1)} %param.9, bf16[384,2,7168]{2,1,0:T(2,128)(2,1)S(1)} %bitcast.25), kind=kOutput, calls=%fused_computation.8 | convolution fusion | flops 2818572288 | bytes 19136512 | tf_op jit(solution)/shard_map/red,edf->ref/dot_general | solution.py:38
  152.2 6.1 %fusion.13 = bf16[384,2,256]{2,0,1:T(8,128)(2,1)S(1)} fusion(bf16[2,7168,256]{2,1,0:T(8,128)(2,1)} %param.10, bf16[384,2,7168]{2,1,0:T(2,128)(2,1)S(1)} %bitcast.26, f32[384,2,256]{2,0,1:T(8,128)S(1)} %fusion.4), kind=kOutput, calls=%fused_computation.11 | convolution fusion | flops 2819751936 | bytes 19529728 | tf_op jit(solution)/shard_map/red,edf->ref/dot_general | solution.py:39
  158.3 12.1 %convolution_bitcast_fusion = f32[384,2,7168]{2,0,1:T(8,128)} fusion(bf16[384,2,256]{2,0,1:T(8,128)(2,1)S(1)} %fusion.13, bf16[2,256,7168]{2,1,0:T(8,128)(2,1)} %param.11), kind=kOutput, calls=%fused_computation.1 | convolution fusion | flops 2818572288 | bytes 29753344 | tf_op jit(solution)/shard_map/ref,efd->red/dot_general | solution.py:40
  170.5 37.0 %copy.12 = f32[384,2,7168]{2,1,0:T(2,128)} copy(f32[384,2,7168]{2,0,1:T(8,128)} %convolution_bitcast_fusion) | data formatting | bytes 44040192 | tf_op jit(solution)/shard_map/ref,efd->red/transpose | solution.py:40
  207.5 0.0 copy-start.2
  207.5 7.2 %all-to-all-start.1 = ((f32[128,3,2,7168]{3,2,1,0:T(2,128)}), f32[128,3,2,7168]{3,2,1,0:T(2,128)}, u32[]{:S(2)}, u32[]{:S(2)}) async-start(f32[128,3,2,7168]{3,2,1,0:T(2,128)} %bitcast.23), calls=%async_computation.1 | async-start | bytes 44040192 | tf_op jit(solution)/shard_map/all_to_all | solution.py:47
  214.7 0.0 copy-done.2
  214.7 0.1 select_reduce_fusion
  214.8 333.2 %all-to-all-done.1 = f32[128,3,2,7168]{3,2,1,0:T(2,128)} async-done(((f32[128,3,2,7168]{3,2,1,0:T(2,128)}), f32[128,3,2,7168]{3,2,1,0:T(2,128)}, u32[]{:S(2)}, u32[]{:S(2)}) %all-to-all-start.1) | async-done | bytes 22020128 | tf_op jit(solution)/shard_map/all_to_all | solution.py:47
  548.0 0.0 copy-start.1
  548.0 10.2 %bitcast_reduce_fusion = f32[16,3,2,7168]{3,2,1,0:T(2,128)S(1)} fusion(f32[128,3,2,7168]{3,2,1,0:T(2,128)} %all-to-all-done.1), kind=kLoop, calls=%fused_computation | loop fusion | flops 4816896 | bytes 24772608 | tf_op jit(solution)/shard_map/reduce_sum | solution.py:51
  558.3 3.0 reshape.84
  561.3 3.8 convolution_convert_fusion.1
  565.1 0.0 copy-done.1
Async XLA Ops:
  0.0 2.0 copy-start
  207.5 7.2 %copy-start.2 = (f32[4,8]{1,0:T(4,128)S(1)}, f32[4,8]{1,0:T(4,128)}, u32[]{:S(2)}) copy-start(f32[4,8]{1,0:T(4,128)} %param.8) | copy-start | bytes 388
  207.5 340.5 %all-to-all-start.1 = ((f32[128,3,2,7168]{3,2,1,0:T(2,128)}), f32[128,3,2,7168]{3,2,1,0:T(2,128)}, u32[]{:S(2)}, u32[]{:S(2)}) async-start(f32[128,3,2,7168]{3,2,1,0:T(2,128)} %bitcast.23), calls=%async_computation.1 | async-start | bytes 44040192 | tf_op jit(solution)/shard_map/all_to_all | solution.py:47
  548.0 17.0 %copy-start.1 = (bf16[4,7168]{1,0:T(4,128)(2,1)S(1)}, bf16[4,7168]{1,0:T(4,128)(2,1)}, u32[]{:S(2)}) copy-start(bf16[4,7168]{1,0:T(4,128)(2,1)} %param.6) | copy-start | bytes 172036
where the time goes:
time: 565 us
  waiting for transfers between devices  333 us (59%)
  blocking collectives  136 us (24%)
  local copies, waits for them, and re-layouts  47.6 us (8%)
  matrix products  29.3 us (5%)
  other arithmetic  11.4 us (2%)
  starting transfers between devices  7.23 us (1%)
    all_to_all x1, waiting for transfers between devices, on_device(): lax.all_to_all(partial_value, ('node', 'local'), split_axis=0, concat_axi...  333 us
    all_to_all x1, blocking collectives, on_device(): lax.all_to_all(copies, ('node', 'local'), split_axis=0, concat_axis=1, ti...  136 us
    transpose x1, local copies, waits for them, and re-layouts, on_device(): jnp.einsum('ref,efd->red', (jax.nn.silu(gate_act) * up_act).astype(jnp.bf...  37 us
    dot_general x1, matrix products, on_device(): jnp.einsum('ref,efd->red', (jax.nn.silu(gate_act) * up_act).astype(jnp.bf...  12.1 us
  transfers between devices with their start and end apart: 1, of which 1 were waited for; matrix products, arithmetic and copies ran while one was open for 0% of the time, Pallas kernels for 0%

commit v1 on v0

v1 whole, which is shorter than its diff:
```python
import jax
import jax.numpy as jnp
from jax import lax
from jax.experimental import pallas as pl
from jax.experimental.pallas import tpu as pltpu
from jax.sharding import PartitionSpec as P

MESH = pl.DeviceIdType.MESH
F32, BF16 = jnp.float32, jnp.bfloat16
LANE = 128
HALF = 3584
QUARTER = 1792
TOKENS = 512
WIDE = 640
ORDERS = ("xyz", "yzx", "zxy")
PLACE = {"z": 0, "y": 1, "x": 2}
FORWARD, BACK, FAR = 1, 3, 2
CHUNKS = {"A": (0, 6, (0, 256)), "B": (6, 6, (256, 256)), "C": (12, 2, (512, 128))}
N_SEMS = 240


def coordinates():
    node, local = lax.axis_index("node"), lax.axis_index("local")
    return {"x": local // 2, "y": node // 4, "z": node % 4, "core": local % 2}


def neighbour(axis, step):
    at = coordinates()
    if axis == "core":
        at["core"] = 1 - at["core"]
    else:
        at[axis] = lax.rem(at[axis] + step, 4)
    return (at["y"] * 4 + at["z"], at["x"] * 2 + at["core"])


def place(split, c=slice(None), b=slice(None), a=slice(None)):
    order = ORDERS[split]
    index = [None, None, None]
    for axis, value in zip(order, (a, b, c)):
        index[PLACE[axis]] = value
    return tuple(index)


def plane(split, b=slice(None), a=slice(None)):
    order = ORDERS[split]
    return tuple(v for _, v in sorted([(PLACE[order[0]], a), (PLACE[order[1]], b)], key=lambda p: p[0]))


def tiles_of(chunk, split):
    first, count, _ = CHUNKS[chunk]
    if chunk == "C":
        return (first + split, 1) if split < 2 else None
    return (first + 2 * split, 2)


def kernel(tokens, ids, weights, w_gate, w_up, w_down, out,
           own, sent, got, xs, lhs_a, lhs_b, lhs_c, wgu_a, wgu_b, wgu_c, wd, acc, hid, scale,
           own_sum, other_sum, core_got, r1, r2, r3, r4, fin, fin_got, send_sem, recv_sem, local_sem):
    core = lax.axis_index("local") % 2
    node = lax.axis_index("node")
    used = [0]
    pending = []

    def send(src, dst, axis, step=0):
        i = used[0]
        used[0] += 1
        copy = pltpu.make_async_remote_copy(
            src_ref=src, dst_ref=dst, send_sem=send_sem.at[i], recv_sem=recv_sem.at[i],
            device_id=neighbour(axis, step), device_id_type=MESH)
        copy.start()
        pending.append(copy)
        return copy

    barrier = pltpu.get_barrier_semaphore()
    friends = [(axis, step) for axis in "xyz" for step in (1, 2, 3)] + [("core", 0)]
    for axis, step in friends:
        pl.semaphore_signal(barrier, inc=1, device_id=neighbour(axis, step), device_id_type=MESH)

    fetches = {"A": [], "B": [], "C": [], "D": []}

    def fetch(src, dst, name):
        copy = pltpu.make_async_copy(src, dst, local_sem.at[sum(len(v) for v in fetches.values())])
        copy.start()
        fetches[name].append(copy)

    wgu = {"A": wgu_a, "B": wgu_b, "C": wgu_c}
    lhs = {"A": lhs_a, "B": lhs_b, "C": lhs_c}

    def fetch_chunk(name):
        first, count, _ = CHUNKS[name]
        for which, source in enumerate((w_gate, w_up)):
            for half in range(2):
                side = lax.rem(core + half, 2)
                for h in range(2):
                    start = pl.multiple_of(side * HALF + h * QUARTER + first * LANE, LANE)
                    fetch(source.at[:, pl.ds(start, count * LANE), :],
                          wgu[name].at[2 * which:2 * which + 2, pl.ds((half * 2 + h) * count * LANE, count * LANE), :], name)

    fetch_chunk("A")

    row4 = lax.broadcasted_iota(jnp.int32, (4, LANE), 1)
    dense = jnp.zeros((4, LANE), F32)
    for k in range(8):
        dense = dense + jnp.where(row4 % 32 == ids[:, k:k + 1], weights[:, k:k + 1], 0.0)
    high = dense.astype(BF16).astype(F32)
    mid = (dense - high).astype(BF16).astype(F32)
    low = dense - high - mid
    meta = jnp.where(row4 < 32, high, jnp.where(row4 < 64, mid, jnp.where(row4 < 96, low, 0.0)))
    left = tokens[:, :HALF].astype(F32)
    right = tokens[:, HALF:].astype(F32)
    mine = jnp.where(core == 0, left, right)
    theirs = jnp.where(core == 0, right, left)
    for r in (0, 4):
        own[r:r + 4, :HALF] = mine
        own[r:r + 4, HALF:] = meta
        sent[r:r + 4, :HALF] = theirs
        sent[r:r + 4, HALF:] = meta

    pl.semaphore_wait(barrier, len(friends))

    swap = send(sent, got, "core")
    fetch_chunk("B")
    swap.wait_recv()
    block = jnp.where(lax.broadcasted_iota(jnp.int32, (8, HALF + LANE), 0) // 4 == core, own[...], got[...])
    for split in range(3):
        for name, (_, _, (at, width)) in CHUNKS.items():
            span = tiles_of(name, split)
            if span is None:
                piece = jnp.concatenate([block[:, HALF:], block[:, HALF:]], axis=0)
            else:
                lo = span[0] * LANE
                piece = jnp.concatenate([block[:, lo:lo + width], block[:, QUARTER + lo:QUARTER + lo + width]], axis=0)
            xs[0, split, 0, 0, 0, :, at:at + width] = piece.astype(BF16)

    def xref(half, split, c, b=slice(None), a=slice(None), cols=None):
        index = (half, split) + place(split, c, b, a)
        if cols is not None:
            index = index + (slice(None), pl.ds(*cols))
        return xs.at[index]

    first, second = {}, {}
    for split in range(3):
        axis = ORDERS[split][0]
        first[split] = [send(xref(0, split, 0, 0, 0), xref(0, split, 0, 0, (4 - step) % 4), axis, step) for step in (1, 3, 2)]
    fetch_chunk("C")
    for half in range(2):
        side = lax.rem(core + half, 2)
        fetch(w_down.at[:, :, pl.ds(pl.multiple_of(side * HALF, LANE), HALF)], wd.at[half], "D")
    for split in range(3):
        axis = ORDERS[split][1]
        for copy in first[split]:
            copy.wait_recv()
        second[split] = [send(xref(0, split, 0, 0), xref(0, split, 0, (4 - step) % 4), axis, step) for step in (1, 3, 2)]

    third, passed, crossed = {}, {}, {}

    def spread(name, split):
        cols = CHUNKS[name][2]
        axis = ORDERS[split][2]
        third[name, split] = (
            send(xref(0, split, 0, cols=cols), xref(0, split, BACK, cols=cols), axis, 1),
            send(xref(0, split, 0, cols=cols), xref(0, split, FORWARD, cols=cols), axis, 3))

    def pass_on(name, split):
        cols = CHUNKS[name][2]
        axis = ORDERS[split][2]
        lower, upper = slice(0, 2), slice(2, 4)
        from_back, from_forward = third[name, split]
        from_back.wait_recv()
        one = send(xref(0, split, BACK, lower, cols=cols), xref(0, split, FAR, lower, cols=cols), axis, 1)
        from_forward.wait_recv()
        two = send(xref(0, split, FORWARD, upper, cols=cols), xref(0, split, FAR, upper, cols=cols), axis, 3)
        passed[name, split] = (one, two)
        crossed[name, split] = [
            send(xref(0, split, c, cols=cols), xref(1, split, c, cols=cols), "core") for c in (BACK, FORWARD)]

    def cross_far(name, split):
        cols = CHUNKS[name][2]
        for copy in passed[name, split]:
            copy.wait_recv()
        crossed[name, split].append(send(xref(0, split, FAR, cols=cols), xref(1, split, FAR, cols=cols), "core"))

    near = []
    for split in range(3):
        for copy in second[split]:
            copy.wait_recv()
        spread("A", split)
    for split in range(3):
        spread("B", split)
    for split in range(3):
        near.append(send(xref(0, split, 0), xref(1, split, 0), "core"))
    for split in range(3):
        spread("C", split)

    def relayout(name):
        first_tile, count, (at, width) = CHUNKS[name]
        for half in range(2):
            for split in range(3):
                span = tiles_of(name, split)
                if span is None:
                    continue

                def rows(z, _, half=half, split=split, span=span):
                    v = xs[half, split, z, :, :, :, at:at + width].astype(F32).reshape(16, 2, 8, width)
                    for h in range(2):
                        col = ((half * 2 + h) * count + span[0] - first_tile) * LANE
                        lhs[name][pl.ds(z * 128, 128), col:col + width] = v[:, h].reshape(128, width).astype(BF16)
                    return 0

                lax.fori_loop(0, 4, rows, 0)

    def multiply(name, start):
        for copy in fetches[name]:
            copy.wait()

        def one(i, _):
            product = jnp.dot(lhs[name][...], wgu[name][i], preferred_element_type=F32)
            if start:
                acc[i] = product
            else:
                acc[i] += product
            return 0

        lax.fori_loop(0, 4, one, 0)

    def arrive(name):
        for split in range(3):
            for copy in crossed[name, split]:
                copy.wait_recv()

    for split in range(3):
        pass_on("A", split)
    for split in range(3):
        pass_on("B", split)
    for split in range(3):
        cross_far("A", split)
    for copy in near:
        copy.wait_recv()
    arrive("A")
    relayout("A")
    multiply("A", True)
    for split in range(3):
        pass_on("C", split)
    for split in range(3):
        cross_far("B", split)
    arrive("B")
    relayout("B")
    multiply("B", False)
    for split in range(3):
        cross_far("C", split)
    arrive("C")
    relayout("C")
    multiply("C", False)

    lane = lax.broadcasted_iota(jnp.int32, (128, LANE), 1)

    def weigh(z, _):
        v = xs[0, 2, z, :, :, :, 512:640].astype(F32).reshape(16, 2, 8, LANE)[:, 0].reshape(128, LANE)
        for e in range(2):
            w = jnp.sum(jnp.where(lane % 32 == node * 2 + e, v, 0.0), axis=1, keepdims=True)
            scale[e, pl.ds(z * 128, 128), :] = jnp.broadcast_to(w, (128, 256))
        return 0

    lax.fori_loop(0, 4, weigh, 0)

    def activate(i, _):
        rows = pl.ds(i * 128, 128)
        for e in range(2):
            gate = acc[e, rows, :]
            hid[e, rows, :] = (gate / (1.0 + jnp.exp(-gate)) * acc[2 + e, rows, :]).astype(BF16)
        return 0

    lax.fori_loop(0, 4, activate, 0)

    for copy in fetches["D"]:
        copy.wait()

    def project(name, half, target):
        first_tile, count, (at, width) = CHUNKS[name]
        for pair in range(count // 2):
            lo = (first_tile + 2 * pair) * LANE

            def rows(m, _, lo=lo, pair=pair):
                part = pl.ds(m * 256, 256)
                parts = []
                for h in range(2):
                    cols = slice(h * QUARTER + lo, h * QUARTER + lo + 256)
                    y = scale[0, part, :] * jnp.dot(hid[0, part, :], wd[half, 0, :, cols], preferred_element_type=F32)
                    y = y + scale[1, part, :] * jnp.dot(hid[1, part, :], wd[half, 1, :, cols], preferred_element_type=F32)
                    parts.append(y.reshape(32, 8, 256))
                block = jnp.concatenate(parts, axis=1).astype(BF16).reshape(2, 4, 4, 16, 256)
                if name == "C":
                    target[0, pl.ds(m * 2, 2), :, :, :, at:at + width] = block[..., :LANE]
                    target[1, pl.ds(m * 2, 2), :, :, :, at:at + width] = block[..., LANE:]
                else:
                    target[pair, pl.ds(m * 2, 2), :, :, :, at:at + width] = block
                return 0

            lax.fori_loop(0, 2, rows, 0)

    def splits_of(name):
        return (0, 1) if name == "C" else (0, 1, 2)

    def ref_of(array, name, index):
        return array.at[index + (slice(None), pl.ds(*CHUNKS[name][2]))]

    swaps, early, late, rowed, single = {}, {}, {}, {}, {}

    def produce(name):
        project(name, 1, other_sum)
        swaps[name] = [
            send(ref_of(other_sum, name, (split,) + place(split)), ref_of(core_got, name, (split,) + place(split)), "core")
            for split in splits_of(name)]
        project(name, 0, own_sum)

    lower, upper = slice(0, 2), slice(2, 4)

    def add(name, target, extras):
        cols = pl.ds(*CHUNKS[name][2])
        total = target[0][target[1] + (slice(None), cols)].astype(F32)
        for array, index in extras:
            total = total + array[index + (slice(None), cols)].astype(F32)
        target[0][target[1] + (slice(None), cols)] = total.astype(BF16)

    def reduce_cores(name):
        cols = pl.ds(*CHUNKS[name][2])
        for copy, split in zip(swaps[name], splits_of(name)):
            copy.wait_recv()

            def slab(z, _, split=split):
                add(name, (own_sum, (split, z, slice(None), slice(None))), [(core_got, (split, z, slice(None), slice(None)))])
                return 0

            lax.fori_loop(0, 4, slab, 0)
            axis = ORDERS[split][2]
            to_forward = send(ref_of(own_sum, name, (split,) + place(split, FAR, lower)),
                              ref_of(r1, name, (split,) + plane(split, lower)), axis, 1)
            to_back = send(ref_of(own_sum, name, (split,) + place(split, FAR, upper)),
                           ref_of(r1, name, (split,) + plane(split, upper)), axis, 3)
            half_one = send(ref_of(own_sum, name, (split,) + place(split, FORWARD, upper)),
                            ref_of(r2, name, (split, 0) + plane(split, upper)), axis, 1)
            half_two = send(ref_of(own_sum, name, (split,) + place(split, BACK, lower)),
                            ref_of(r2, name, (split, 1) + plane(split, lower)), axis, 3)
            early[name, split] = (to_forward, to_back, half_one, half_two)

    def reduce_far(name):
        for split in splits_of(name):
            axis = ORDERS[split][2]
            to_forward, to_back, _, _ = early[name, split]
            to_forward.wait_recv()
            add(name, (own_sum, (split,) + place(split, FORWARD, lower)), [(r1, (split,) + plane(split, lower))])
            one = send(ref_of(own_sum, name, (split,) + place(split, FORWARD, lower)),
                       ref_of(r2, name, (split, 0) + plane(split, lower)), axis, 1)
            to_back.wait_recv()
            add(name, (own_sum, (split,) + place(split, BACK, upper)), [(r1, (split,) + plane(split, upper))])
            two = send(ref_of(own_sum, name, (split,) + place(split, BACK, upper)),
                       ref_of(r2, name, (split, 1) + plane(split, upper)), axis, 3)
            late[name, split] = (one, two)

    def reduce_plane(name):
        for split in splits_of(name):
            for copy in early[name, split][2:] + late[name, split]:
                copy.wait_recv()
            add(name, (own_sum, (split,) + place(split, 0)),
                [(r2, (split, 0) + plane(split)), (r2, (split, 1) + plane(split))])
            rowed[name, split] = [
                send(ref_of(own_sum, name, (split,) + place(split, 0, step)), ref_of(r3, name, (split, step, slice(None))), ORDERS[split][1], step)
                for step in (1, 3, 2)]

    def reduce_row(name):
        for split in splits_of(name):
            for copy in rowed[name, split]:
                copy.wait_recv()
            add(name, (own_sum, (split,) + place(split, 0, 0)), [(r3, (split, step, slice(None))) for step in (1, 2, 3)])
            single[name, split] = [
                send(ref_of(own_sum, name, (split,) + place(split, 0, 0, step)), ref_of(r4, name, (split, step)), ORDERS[split][0], step)
                for step in (1, 3, 2)]

    def reduce_last(name):
        cols = pl.ds(*CHUNKS[name][2])
        for split in splits_of(name):
            for copy in single[name, split]:
                copy.wait_recv()
            total = own_sum[split, 0, 0, 0, :, cols].astype(F32)
            for step in (1, 2, 3):
                total = total + r4[split, step, :, cols].astype(F32)
            fin[split, :, cols] = total.astype(BF16)

    produce("C")
    reduce_cores("C")
    produce("A")
    reduce_cores("A")
    reduce_far("C")
    produce("B")
    reduce_cores("B")
    reduce_far("A")
    reduce_plane("C")
    reduce_far("B")
    reduce_plane("A")
    reduce_row("C")
    reduce_plane("B")
    reduce_row("A")
    reduce_last("C")
    reduce_row("B")
    reduce_last("A")
    reduce_last("B")

    back = send(fin, fin_got, "core")
    back.wait_recv()
    for split in range(3):
        for name, (_, _, (at, width)) in CHUNKS.items():
            span = tiles_of(name, split)
            if span is None:
                continue
            a = fin[split, :, at:at + width].astype(F32)
            b = fin_got[split, :, at:at + width].astype(F32)
            for half in range(2):
                v = jnp.where(core == half, a, b)
                for h in range(2):
                    col = half * HALF + h * QUARTER + span[0] * LANE
                    rows = jnp.where(core == 0, v[8 * h:8 * h + 4], v[8 * h + 4:8 * h + 8])
                    out[:, col:col + width] = rows.astype(BF16)
    for copy in pending:
        copy.wait_send()


def on_device(tokens, expert_ids, route_weights, w_gate, w_up, w_down):
    vmem = pl.BlockSpec(memory_space=pltpu.VMEM)
    anywhere = pl.BlockSpec(memory_space=pl.ANY)
    grid3 = (3, 4, 4, 4, 16, WIDE)
    return pl.pallas_call(
        kernel,
        out_shape=jax.ShapeDtypeStruct((4, 7168), BF16),
        in_specs=[vmem, vmem, vmem, anywhere, anywhere, anywhere],
        out_specs=vmem,
        scratch_shapes=[
            pltpu.VMEM((8, HALF + LANE), F32),
            pltpu.VMEM((8, HALF + LANE), F32),
            pltpu.VMEM((8, HALF + LANE), F32),
            pltpu.VMEM((2,) + grid3, BF16),
            pltpu.VMEM((TOKENS, 24 * LANE), BF16),
            pltpu.VMEM((TOKENS, 24 * LANE), BF16),
            pltpu.VMEM((TOKENS, 8 * LANE), BF16),
            pltpu.VMEM((4, 24 * LANE, 256), BF16),
            pltpu.VMEM((4, 24 * LANE, 256), BF16),
            pltpu.VMEM((4, 8 * LANE, 256), BF16),
            pltpu.VMEM((2, 2, 256, HALF), BF16),
            pltpu.VMEM((4, TOKENS, 256), F32),
            pltpu.VMEM((2, TOKENS, 256), BF16),
            pltpu.VMEM((2, TOKENS, 256), F32),
            pltpu.VMEM(grid3, BF16),
            pltpu.VMEM(grid3, BF16),
            pltpu.VMEM(grid3, BF16),
            pltpu.VMEM((3, 4, 4, 16, WIDE), BF16),
            pltpu.VMEM((3, 2, 4, 4, 16, WIDE), BF16),
            pltpu.VMEM((3, 4, 4, 16, WIDE), BF16),
            pltpu.VMEM((3, 4, 16, WIDE), BF16),
            pltpu.VMEM((3, 16, WIDE), BF16),
            pltpu.VMEM((3, 16, WIDE), BF16),
            pltpu.SemaphoreType.DMA((N_SEMS,)),
            pltpu.SemaphoreType.DMA((N_SEMS,)),
            pltpu.SemaphoreType.DMA((32,)),
        ],
        compiler_params=pltpu.CompilerParams(
            collective_id=0, has_side_effects=True, vmem_limit_bytes=62 * 2**20),
        cost_estimate=pl.CostEstimate(flops=11_300_000_000, bytes_accessed=22_100_000, transcendentals=262_144),
    )(tokens, expert_ids, route_weights, w_gate, w_up, w_down)


def solution(mesh):
    placed = (
        P(("node", "local"), None),
        P(("node", "local"), None),
        P(("node", "local"), None),
        P("node", None, "local"),
        P("node", None, "local"),
        P("node", "local", None),
    )
    return jax.shard_map(
        on_device, mesh=mesh, in_specs=placed, out_specs=P(("node", "local"), None), check_vma=False
    )
```

time: 565 us -> 84 us (0.15)
  the two profiles are of different devices: /device:TPU:10 before, /device:TPU:1 now
where the time goes in v1:
time: 84 us; the launch traced here: 83.8 us
  Pallas kernels  82.3 us (98%)
  local copies, waits for them, and re-layouts  1.46 us (2%)
    pallas_call x1, Pallas kernels, on_device(): pl.pallas_call(kernel, out_shape=jax.ShapeDtypeStruct((4, 7168), BF16), i...  82.3 us

profile of v1, /device:TPU:1, one launch (start us, length us, event | category | flops | bytes accessed | tf_op | source)
XLA Modules:
  0.0 83.8 jit_solution(13111730483580119978)
XLA Ops:
  0.0 82.3 %shard_map.64 = bf16[4,7168]{1,0:T(4,128)(2,1)} custom-call(bf16[4,7168]{1,0:T(4,128)(2,1)} %tokens.1, s32[4,8]{1,0:T(4,128)} %ids.1, f32[4,8]{1,0:T(4,128)} %weights.1, bf16[2,7168,256]{2,1,0:T(8,128)(2,1)} %w_gate.1, bf16[2,7168,256]{2,1,0:T(8,128)(2,1)} %w_up.1, bf16[2,256,7168]{2,1,0:T(8,128)(2,1)} %w_down.1), custom_call_target="tpu_custom_call" | custom-call | flops 11299999744 | bytes 22100000 | tf_op jit(solution)/shard_map/pallas_call | solution.py:431
  82.3 1.5 %copy.8 = bf16[4,7168]{1,0:T(4,128)(2,1)} copy(bf16[4,7168]{1,0:T(4,128)(2,1)} %shard_map.64) | data formatting | bytes 114688

commit v2 on v1

v2 whole, which is shorter than its diff:
```python
import jax
import jax.numpy as jnp
from jax import lax
from jax.experimental import pallas as pl
from jax.experimental.pallas import tpu as pltpu
from jax.sharding import PartitionSpec as P

MESH = pl.DeviceIdType.MESH
F32, BF16 = jnp.float32, jnp.bfloat16
LANE = 128
HALF = 3584
QUARTER = 1792
TOKENS = 512
WIDE = 640
ORDERS = ("xyz", "yzx", "zxy")
PLACE = {"z": 0, "y": 1, "x": 2}
FORWARD, BACK, FAR = 1, 3, 2
CHUNKS = {"A": (0, 6, (0, 256)), "B": (6, 6, (256, 256)), "C": (12, 2, (512, 128))}
N_SEND, N_RECV = 24, 80


def coordinates():
    node, local = lax.axis_index("node"), lax.axis_index("local")
    return {"x": local // 2, "y": node // 4, "z": node % 4, "core": local % 2}


def neighbour(axis, step):
    at = coordinates()
    if axis == "core":
        at["core"] = 1 - at["core"]
    else:
        at[axis] = lax.rem(at[axis] + step, 4)
    return (at["y"] * 4 + at["z"], at["x"] * 2 + at["core"])


def place(split, c=slice(None), b=slice(None), a=slice(None)):
    order = ORDERS[split]
    index = [None, None, None]
    for axis, value in zip(order, (a, b, c)):
        index[PLACE[axis]] = value
    return tuple(index)


def plane(split, b=slice(None), a=slice(None)):
    order = ORDERS[split]
    return tuple(v for _, v in sorted([(PLACE[order[0]], a), (PLACE[order[1]], b)], key=lambda p: p[0]))


def tiles_of(chunk, split):
    first, count, _ = CHUNKS[chunk]
    if chunk == "C":
        return (first + split, 1) if split < 2 else None
    return (first + 2 * split, 2)


def kernel(tokens, ids, weights, w_gate, w_up, w_down, out,
           own, sent, got, xs, lhs_a, lhs_b, lhs_c, wgu_a, wgu_b, wgu_c, wd, acc, hid, scale,
           own_sum, other_sum, core_got, r1, r2, r3, r4, fin, fin_got, send_sem, recv_sem, local_sem):
    core = lax.axis_index("local") % 2
    node = lax.axis_index("node")
    send_slots, recv_slots, send_totals = {}, {}, {}

    def slot(table, key):
        return table.setdefault(key, len(table))

    def send(src, dst, axis, step, recv_key, send_key):
        copy = pltpu.make_async_remote_copy(
            src_ref=src, dst_ref=dst, send_sem=send_sem.at[slot(send_slots, send_key)],
            recv_sem=recv_sem.at[slot(recv_slots, recv_key)],
            device_id=neighbour(axis, step), device_id_type=MESH)
        copy.start()

    def received(key, ref):
        pltpu.make_async_copy(ref, ref, recv_sem.at[recv_slots[key]]).wait()

    def all_sent(key, ref):
        pltpu.make_async_copy(ref, ref, send_sem.at[send_slots[key]]).wait()

    barrier = pltpu.get_barrier_semaphore()
    friends = [(axis, step) for axis in "xyz" for step in (1, 2, 3)] + [("core", 0)]
    for axis, step in friends:
        pl.semaphore_signal(barrier, inc=1, device_id=neighbour(axis, step), device_id_type=MESH)

    def fetch(src, dst, i):
        pltpu.make_async_copy(src, dst, local_sem.at[i]).start()

    def fetched(ref, i):
        pltpu.make_async_copy(ref, ref, local_sem.at[i]).wait()

    wgu = {"A": wgu_a, "B": wgu_b, "C": wgu_c}
    lhs = {"A": lhs_a, "B": lhs_b, "C": lhs_c}

    def fetch_chunk(name):
        first, count, _ = CHUNKS[name]
        for which, source in enumerate((w_gate, w_up)):
            for half in range(2):
                side = lax.rem(core + half, 2)
                for h in range(2):
                    start = pl.multiple_of(side * HALF + h * QUARTER + first * LANE, LANE)
                    fetch(source.at[:, pl.ds(start, count * LANE), :],
                          wgu[name].at[2 * which:2 * which + 2, pl.ds((half * 2 + h) * count * LANE, count * LANE), :], "ABC".index(name))

    fetch_chunk("A")

    row4 = lax.broadcasted_iota(jnp.int32, (4, LANE), 1)
    dense = jnp.zeros((4, LANE), F32)
    for k in range(8):
        dense = dense + jnp.where(row4 % 32 == ids[:, k:k + 1], weights[:, k:k + 1], 0.0)
    high = dense.astype(BF16).astype(F32)
    mid = (dense - high).astype(BF16).astype(F32)
    low = dense - high - mid
    meta = jnp.where(row4 < 32, high, jnp.where(row4 < 64, mid, jnp.where(row4 < 96, low, 0.0)))
    left = tokens[:, :HALF].astype(F32)
    right = tokens[:, HALF:].astype(F32)
    mine = jnp.where(core == 0, left, right)
    theirs = jnp.where(core == 0, right, left)
    for r in (0, 4):
        own[r:r + 4, :HALF] = mine
        own[r:r + 4, HALF:] = meta
        sent[r:r + 4, :HALF] = theirs
        sent[r:r + 4, HALF:] = meta

    pl.semaphore_wait(barrier, len(friends))

    send(sent, got, "core", 0, "entry", "entry")
    fetch_chunk("B")
    received("entry", got)
    block = jnp.where(lax.broadcasted_iota(jnp.int32, (8, HALF + LANE), 0) // 4 == core, own[...], got[...])
    for split in range(3):
        for name, (_, _, (at, width)) in CHUNKS.items():
            span = tiles_of(name, split)
            if span is None:
                piece = jnp.concatenate([block[:, HALF:], block[:, HALF:]], axis=0)
            else:
                lo = span[0] * LANE
                piece = jnp.concatenate([block[:, lo:lo + width], block[:, QUARTER + lo:QUARTER + lo + width]], axis=0)
            xs[0, split, 0, 0, 0, :, at:at + width] = piece.astype(BF16)

    def xref(half, split, c, b=slice(None), a=slice(None), cols=None):
        index = (half, split) + place(split, c, b, a)
        if cols is not None:
            index = index + (slice(None), pl.ds(*cols))
        return xs.at[index]

    for split in range(3):
        for step in (1, 3, 2):
            send(xref(0, split, 0, 0, 0), xref(0, split, 0, 0, (4 - step) % 4), ORDERS[split][0], step, ("first", split), "first")
    fetch_chunk("C")
    for half in range(2):
        side = lax.rem(core + half, 2)
        fetch(w_down.at[:, :, pl.ds(pl.multiple_of(side * HALF, LANE), HALF)], wd.at[half], 3)
    parts = ((0, 256), (256, 384))
    for split in range(3):
        received(("first", split), xref(0, split, 0, 0, slice(1, 4)))
        for part, cols in enumerate(parts):
            for step in (1, 3, 2):
                send(xref(0, split, 0, 0, cols=cols), xref(0, split, 0, (4 - step) % 4, cols=cols), ORDERS[split][1], step,
                     ("second", part, split), ("second", part))

    lower, upper = slice(0, 2), slice(2, 4)

    def spread(name, split):
        cols = CHUNKS[name][2]
        axis = ORDERS[split][2]
        send(xref(0, split, 0, cols=cols), xref(0, split, BACK, cols=cols), axis, 1, ("third", BACK, name, split), "third")
        send(xref(0, split, 0, cols=cols), xref(0, split, FORWARD, cols=cols), axis, 3, ("third", FORWARD, name, split), "third")

    def pass_on(name):
        cols = CHUNKS[name][2]
        for split in range(3):
            axis = ORDERS[split][2]
            for side, part, step in ((BACK, lower, 1), (FORWARD, upper, 3)):
                received(("third", side, name, split), xref(0, split, side, cols=cols))
                send(xref(0, split, side, part, cols=cols), xref(0, split, FAR, part, cols=cols), axis, step,
                     ("passed", name, split), "passed")
                send(xref(0, split, side, cols=cols), xref(1, split, side, cols=cols), "core", 0, ("cross", name), "cross")

    def cross_far(name):
        cols = CHUNKS[name][2]
        for split in range(3):
            received(("passed", name, split), xref(0, split, FAR, cols=cols))
            send(xref(0, split, FAR, cols=cols), xref(1, split, FAR, cols=cols), "core", 0, ("cross", name), "cross")

    def arrive(name):
        received(("cross", name), xs.at[1, :, 1:4, :, :, :, pl.ds(*CHUNKS[name][2])])

    for part, names in ((0, "A"), (1, "BC")):
        for split in range(3):
            received(("second", part, split), xref(0, split, 0, slice(1, 4), cols=parts[part]))
            for name in names:
                spread(name, split)
    for split in range(3):
        send(xref(0, split, 0), xref(1, split, 0), "core", 0, "near", "near")

    def relayout(name):
        first_tile, count, (at, width) = CHUNKS[name]
        for half in range(2):
            for split in range(3):
                span = tiles_of(name, split)
                if span is None:
                    continue

                def rows(z, _, half=half, split=split, span=span):
                    v = xs[half, split, z, :, :, :, at:at + width].astype(F32).reshape(16, 2, 8, width)
                    for h in range(2):
                        col = ((half * 2 + h) * count + span[0] - first_tile) * LANE
                        lhs[name][pl.ds(z * 128, 128), col:col + width] = v[:, h].reshape(128, width).astype(BF16)
                    return 0

                lax.fori_loop(0, 4, rows, 0)

    def multiply(name, begin, end):
        if begin == 0:
            fetched(wgu[name], "ABC".index(name))

        def one(i, _):
            product = jnp.dot(lhs[name][...], wgu[name][i], preferred_element_type=F32)
            if name == "A":
                acc[i] = product
            else:
                acc[i] += product
            return 0

        lax.fori_loop(begin, end, one, 0)

    pass_on("A")
    pass_on("B")
    cross_far("A")
    received("near", xs.at[1, :, 0])
    arrive("A")
    relayout("A")
    multiply("A", 0, 1)
    pass_on("C")
    multiply("A", 1, 2)
    cross_far("B")
    multiply("A", 2, 4)
    cross_far("C")
    arrive("B")
    relayout("B")
    multiply("B", 0, 4)
    arrive("C")
    relayout("C")
    multiply("C", 0, 4)

    lane = lax.broadcasted_iota(jnp.int32, (128, LANE), 1)

    def weigh(z, _):
        v = xs[0, 2, z, :, :, :, 512:640].astype(F32).reshape(16, 2, 8, LANE)[:, 0].reshape(128, LANE)
        for e in range(2):
            w = jnp.sum(jnp.where(lane % 32 == node * 2 + e, v, 0.0), axis=1, keepdims=True)
            scale[e, pl.ds(z * 128, 128), :] = jnp.broadcast_to(w, (128, 256))
        return 0

    lax.fori_loop(0, 4, weigh, 0)

    def activate(i, _):
        rows = pl.ds(i * 128, 128)
        for e in range(2):
            gate = acc[e, rows, :]
            hid[e, rows, :] = (gate / (1.0 + jnp.exp(-gate)) * acc[2 + e, rows, :]).astype(BF16)
        return 0

    lax.fori_loop(0, 4, activate, 0)

    fetched(wd, 3)

    def project(name, half, target):
        first_tile, count, (at, width) = CHUNKS[name]
        for pair in range(count // 2):
            lo = (first_tile + 2 * pair) * LANE

            halves = []
            for h in range(2):
                cols = slice(h * QUARTER + lo, h * QUARTER + lo + 256)
                y = scale[0] * jnp.dot(hid[0], wd[half, 0, :, cols], preferred_element_type=F32)
                y = y + scale[1] * jnp.dot(hid[1], wd[half, 1, :, cols], preferred_element_type=F32)
                halves.append(y.reshape(64, 8, 256))
            block = jnp.concatenate(halves, axis=1).astype(BF16).reshape(4, 4, 4, 16, 256)
            if name == "C":
                target[0, :, :, :, :, at:at + width] = block[..., :LANE]
                target[1, :, :, :, :, at:at + width] = block[..., LANE:]
            else:
                target[pair, :, :, :, :, at:at + width] = block

    def splits_of(name):
        return (0, 1) if name == "C" else (0, 1, 2)

    def ref_of(array, name, index):
        return array.at[index + (slice(None), pl.ds(*CHUNKS[name][2]))]

    def produce_other(name):
        project(name, 1, other_sum)
        for split in splits_of(name):
            send(ref_of(other_sum, name, (split,) + place(split)), ref_of(core_got, name, (split,) + place(split)), "core", 0,
                 ("swap", name), ("swap", name))

    def produce_own(name):
        project(name, 0, own_sum)

    def group(array, name, index=()):
        some = slice(0, len(splits_of(name)))
        return array.at[(some,) + index + (slice(None),) * (len(array.shape) - len(index) - 2) + (pl.ds(*CHUNKS[name][2]),)]

    def add(name, target, extras):
        cols = pl.ds(*CHUNKS[name][2])
        total = target[0][target[1] + (slice(None), cols)].astype(F32)
        for array, index in extras:
            total = total + array[index + (slice(None), cols)].astype(F32)
        target[0][target[1] + (slice(None), cols)] = total.astype(BF16)

    def reduce_cores(name):
        received(("swap", name), group(core_got, name))
        for split in splits_of(name):

            def slab(z, _, split=split):
                add(name, (own_sum, (split, z, slice(None), slice(None))), [(core_got, (split, z, slice(None), slice(None)))])
                return 0

            lax.fori_loop(0, 4, slab, 0)
            axis = ORDERS[split][2]
            for part, step in ((lower, 1), (upper, 3)):
                send(ref_of(own_sum, name, (split,) + place(split, FAR, part)), ref_of(r1, name, (split,) + plane(split, part)),
                     axis, step, ("far", step, name, split), ("far", name))
            for side, part, step, way in ((FORWARD, upper, 1, 0), (BACK, lower, 3, 1)):
                send(ref_of(own_sum, name, (split,) + place(split, side, part)),
                     ref_of(r2, name, (split, way) + plane(split, part)), axis, step, ("sides", name, split), ("sides", name))

    def reduce_far(name):
        for split in splits_of(name):
            axis = ORDERS[split][2]
            for side, part, step, way in ((FORWARD, lower, 1, 0), (BACK, upper, 3, 1)):
                received(("far", step, name, split), ref_of(r1, name, (split,) + plane(split, part)))
                add(name, (own_sum, (split,) + place(split, side, part)), [(r1, (split,) + plane(split, part))])
                send(ref_of(own_sum, name, (split,) + place(split, side, part)),
                     ref_of(r2, name, (split, way) + plane(split, part)), axis, step, ("sides", name, split), ("sides", name))

    def reduce_plane(name):
        for split in splits_of(name):
            received(("sides", name, split), ref_of(r2, name, (split,) + (slice(None),) * 3))
            add(name, (own_sum, (split,) + place(split, 0)),
                [(r2, (split, 0) + plane(split)), (r2, (split, 1) + plane(split))])
            for step in (1, 3, 2):
                send(ref_of(own_sum, name, (split,) + place(split, 0, step)), ref_of(r3, name, (split, step, slice(None))),
                     ORDERS[split][1], step, ("row", name, split), ("row", name))

    def reduce_row(name):
        for split in splits_of(name):
            received(("row", name, split), ref_of(r3, name, (split, slice(1, 4), slice(None))))
            add(name, (own_sum, (split,) + place(split, 0, 0)), [(r3, (split, step, slice(None))) for step in (1, 2, 3)])
            for step in (1, 3, 2):
                send(ref_of(own_sum, name, (split,) + place(split, 0, 0, step)), ref_of(r4, name, (split, step)),
                     ORDERS[split][0], step, ("one", name), ("one", name))

    def reduce_last(name):
        cols = pl.ds(*CHUNKS[name][2])
        received(("one", name), group(r4, name, (slice(1, 4),)))
        for split in splits_of(name):
            total = own_sum[split, 0, 0, 0, :, cols].astype(F32)
            for step in (1, 2, 3):
                total = total + r4[split, step, :, cols].astype(F32)
            fin[split, :, cols] = total.astype(BF16)

    produce_other("C")
    produce_own("C")
    produce_other("A")
    reduce_cores("C")
    produce_own("A")
    reduce_cores("A")
    produce_other("B")
    reduce_far("C")
    produce_own("B")
    reduce_cores("B")
    reduce_plane("C")
    reduce_far("A")
    reduce_row("C")
    reduce_far("B")
    reduce_plane("A")
    reduce_last("C")
    reduce_plane("B")
    reduce_row("A")
    reduce_row("B")
    reduce_last("A")
    reduce_last("B")

    send(fin, fin_got, "core", 0, "last", "last")
    received("last", fin_got)
    for split in range(3):
        for name, (_, _, (at, width)) in CHUNKS.items():
            span = tiles_of(name, split)
            if span is None:
                continue
            a = fin[split, :, at:at + width].astype(F32)
            b = fin_got[split, :, at:at + width].astype(F32)
            for half in range(2):
                v = jnp.where(core == half, a, b)
                for h in range(2):
                    col = half * HALF + h * QUARTER + span[0] * LANE
                    rows = jnp.where(core == 0, v[8 * h:8 * h + 4], v[8 * h + 4:8 * h + 8])
                    out[:, col:col + width] = rows.astype(BF16)
    all_sent("entry", got)
    all_sent("first", xs.at[0, :, 0, 0, 1:4])
    for part, cols in enumerate(parts):
        all_sent(("second", part), xs.at[0, :, 0, 1:4, :, :, pl.ds(*cols)])
    all_sent("third", xs.at[0, :, 1:3])
    all_sent("passed", xs.at[0, :, 1])
    all_sent("near", xs.at[1, :, 0])
    all_sent("cross", xs.at[1, :, 1:4])
    for name in CHUNKS:
        all_sent(("swap", name), group(core_got, name))
        all_sent(("far", name), group(r1, name))
        all_sent(("sides", name), group(r2, name))
        all_sent(("row", name), group(r3, name, (slice(1, 4),)))
        all_sent(("one", name), group(r4, name, (slice(1, 4),)))
    all_sent("last", fin_got)


def on_device(tokens, expert_ids, route_weights, w_gate, w_up, w_down):
    vmem = pl.BlockSpec(memory_space=pltpu.VMEM)
    anywhere = pl.BlockSpec(memory_space=pl.ANY)
    grid3 = (3, 4, 4, 4, 16, WIDE)
    return pl.pallas_call(
        kernel,
        out_shape=jax.ShapeDtypeStruct((4, 7168), BF16),
        in_specs=[vmem, vmem, vmem, anywhere, anywhere, anywhere],
        out_specs=vmem,
        scratch_shapes=[
            pltpu.VMEM((8, HALF + LANE), F32),
            pltpu.VMEM((8, HALF + LANE), F32),
            pltpu.VMEM((8, HALF + LANE), F32),
            pltpu.VMEM((2,) + grid3, BF16),
            pltpu.VMEM((TOKENS, 24 * LANE), BF16),
            pltpu.VMEM((TOKENS, 24 * LANE), BF16),
            pltpu.VMEM((TOKENS, 8 * LANE), BF16),
            pltpu.VMEM((4, 24 * LANE, 256), BF16),
            pltpu.VMEM((4, 24 * LANE, 256), BF16),
            pltpu.VMEM((4, 8 * LANE, 256), BF16),
            pltpu.VMEM((2, 2, 256, HALF), BF16),
            pltpu.VMEM((4, TOKENS, 256), F32),
            pltpu.VMEM((2, TOKENS, 256), BF16),
            pltpu.VMEM((2, TOKENS, 256), F32),
            pltpu.VMEM(grid3, BF16),
            pltpu.VMEM(grid3, BF16),
            pltpu.VMEM(grid3, BF16),
            pltpu.VMEM((3, 4, 4, 16, WIDE), BF16),
            pltpu.VMEM((3, 2, 4, 4, 16, WIDE), BF16),
            pltpu.VMEM((3, 4, 4, 16, WIDE), BF16),
            pltpu.VMEM((3, 4, 16, WIDE), BF16),
            pltpu.VMEM((3, 16, WIDE), BF16),
            pltpu.VMEM((3, 16, WIDE), BF16),
            pltpu.SemaphoreType.DMA((N_SEND,)),
            pltpu.SemaphoreType.DMA((N_RECV,)),
            pltpu.SemaphoreType.DMA((4,)),
        ],
        compiler_params=pltpu.CompilerParams(
            collective_id=0, has_side_effects=True, vmem_limit_bytes=62 * 2**20),
        cost_estimate=pl.CostEstimate(flops=11_300_000_000, bytes_accessed=22_100_000, transcendentals=262_144),
    )(tokens, expert_ids, route_weights, w_gate, w_up, w_down)


def solution(mesh):
    placed = (
        P(("node", "local"), None),
        P(("node", "local"), None),
        P(("node", "local"), None),
        P("node", None, "local"),
        P("node", None, "local"),
        P("node", "local", None),
    )
    return jax.shard_map(
        on_device, mesh=mesh, in_specs=placed, out_specs=P(("node", "local"), None), check_vma=False
    )
```

time: 84 us -> 76.1 us (0.906)
  Pallas kernels: 82.3 us -> 74.4 us
    pallas_call x1, Pallas kernels: 82.3 us -> 74.4 us  [on_device(): pl.pallas_call(kernel, out_shape=jax.ShapeDtypeStruct((4, 7168), BF16), i...]
where the time goes in v2:
time: 76.1 us; the launch traced here: 75.9 us
  Pallas kernels  74.4 us (98%)
  local copies, waits for them, and re-layouts  1.46 us (2%)
    pallas_call x1, Pallas kernels, on_device(): pl.pallas_call(kernel, out_shape=jax.ShapeDtypeStruct((4, 7168), BF16), i...  74.4 us

profile of v2, /device:TPU:1, one launch (start us, length us, event | category | flops | bytes accessed | tf_op | source)
XLA Modules:
  0.0 75.9 jit_solution(10435024893431903839)
XLA Ops:
  0.0 74.4 %shard_map.64 = bf16[4,7168]{1,0:T(4,128)(2,1)} custom-call(bf16[4,7168]{1,0:T(4,128)(2,1)} %tokens.1, s32[4,8]{1,0:T(4,128)} %ids.1, f32[4,8]{1,0:T(4,128)} %weights.1, bf16[2,7168,256]{2,1,0:T(8,128)(2,1)} %w_gate.1, bf16[2,7168,256]{2,1,0:T(8,128)(2,1)} %w_up.1, bf16[2,256,7168]{2,1,0:T(8,128)(2,1)} %w_down.1), custom_call_target="tpu_custom_call" | custom-call | flops 11299999744 | bytes 22100000 | tf_op jit(solution)/shard_map/pallas_call | solution.py:421
  74.4 1.5 %copy.8 = bf16[4,7168]{1,0:T(4,128)(2,1)} copy(bf16[4,7168]{1,0:T(4,128)(2,1)} %shard_map.64) | data formatting | bytes 114688

commit v3 on v2

--- a/solution.py
+++ b/solution.py
@@ -16,7 +16,7 @@
 PLACE = {"z": 0, "y": 1, "x": 2}
 FORWARD, BACK, FAR = 1, 3, 2
 CHUNKS = {"A": (0, 6, (0, 256)), "B": (6, 6, (256, 256)), "C": (12, 2, (512, 128))}
-N_SEND, N_RECV = 24, 80
+N_SEND, N_RECV = 22, 85
 
 
 def coordinates():
@@ -149,13 +149,13 @@
     for half in range(2):
         side = lax.rem(core + half, 2)
         fetch(w_down.at[:, :, pl.ds(pl.multiple_of(side * HALF, LANE), HALF)], wd.at[half], 3)
-    parts = ((0, 256), (256, 384))
     for split in range(3):
         received(("first", split), xref(0, split, 0, 0, slice(1, 4)))
-        for part, cols in enumerate(parts):
+        for name in "CAB":
+            cols = CHUNKS[name][2]
             for step in (1, 3, 2):
                 send(xref(0, split, 0, 0, cols=cols), xref(0, split, 0, (4 - step) % 4, cols=cols), ORDERS[split][1], step,
-                     ("second", part, split), ("second", part))
+                     ("second", name, split), "second")
 
     lower, upper = slice(0, 2), slice(2, 4)
 
@@ -181,41 +181,44 @@
             received(("passed", name, split), xref(0, split, FAR, cols=cols))
             send(xref(0, split, FAR, cols=cols), xref(1, split, FAR, cols=cols), "core", 0, ("cross", name), "cross")
 
+    def cross_near(name):
+        cols = CHUNKS[name][2]
+        for split in range(3):
+            send(xref(0, split, 0, cols=cols), xref(1, split, 0, cols=cols), "core", 0, ("cross", name), "cross")
+
     def arrive(name):
-        received(("cross", name), xs.at[1, :, 1:4, :, :, :, pl.ds(*CHUNKS[name][2])])
-
-    for part, names in ((0, "A"), (1, "BC")):
+        received(("cross", name), xs.at[1, :, :, :, :, :, pl.ds(*CHUNKS[name][2])])
+
+    def finish_second(name):
         for split in range(3):
-            received(("second", part, split), xref(0, split, 0, slice(1, 4), cols=parts[part]))
-            for name in names:
-                spread(name, split)
-    for split in range(3):
-        send(xref(0, split, 0), xref(1, split, 0), "core", 0, "near", "near")
-
-    def relayout(name):
+            received(("second", name, split), xref(0, split, 0, slice(1, 4), cols=CHUNKS[name][2]))
+            spread(name, split)
+
+    def relayout(name, half):
         first_tile, count, (at, width) = CHUNKS[name]
-        for half in range(2):
-            for split in range(3):
-                span = tiles_of(name, split)
-                if span is None:
-                    continue
-
-                def rows(z, _, half=half, split=split, span=span):
-                    v = xs[half, split, z, :, :, :, at:at + width].astype(F32).reshape(16, 2, 8, width)
-                    for h in range(2):
-                        col = ((half * 2 + h) * count + span[0] - first_tile) * LANE
-                        lhs[name][pl.ds(z * 128, 128), col:col + width] = v[:, h].reshape(128, width).astype(BF16)
-                    return 0
-
-                lax.fori_loop(0, 4, rows, 0)
-
-    def multiply(name, begin, end):
-        if begin == 0:
+        for split in range(3):
+            span = tiles_of(name, split)
+            if span is None:
+                continue
+
+            def rows(z, _, split=split, span=span):
+                v = xs[half, split, z, :, :, :, at:at + width].astype(F32).reshape(16, 2, 8, width)
+                for h in range(2):
+                    col = ((half * 2 + h) * count + span[0] - first_tile) * LANE
+                    lhs[name][pl.ds(z * 128, 128), col:col + width] = v[:, h].reshape(128, width).astype(BF16)
+                return 0
+
+            lax.fori_loop(0, 4, rows, 0)
+
+    def multiply(name, half, begin, end):
+        if half == 0 and begin == 0:
             fetched(wgu[name], "ABC".index(name))
+        depth = 2 * CHUNKS[name][1] * LANE
+        span = slice(half * depth, half * depth + depth)
 
         def one(i, _):
-            product = jnp.dot(lhs[name][...], wgu[name][i], preferred_element_type=F32)
-            if name == "A":
+            product = jnp.dot(lhs[name][:, span], wgu[name][i, span], preferred_element_type=F32)
+            if name == "C" and half == 0:
                 acc[i] = product
             else:
                 acc[i] += product
@@ -223,24 +226,34 @@
 
         lax.fori_loop(begin, end, one, 0)
 
+    finish_second("C")
+    cross_near("C")
+    finish_second("A")
+    pass_on("C")
+    finish_second("B")
+    cross_near("A")
     pass_on("A")
+    cross_far("C")
+    relayout("C", 0)
+    multiply("C", 0, 0, 4)
+    arrive("C")
+    relayout("C", 1)
+    multiply("C", 1, 0, 4)
     pass_on("B")
     cross_far("A")
-    received("near", xs.at[1, :, 0])
+    cross_near("B")
+    relayout("A", 0)
+    multiply("A", 0, 0, 4)
     arrive("A")
-    relayout("A")
-    multiply("A", 0, 1)
-    pass_on("C")
-    multiply("A", 1, 2)
+    relayout("A", 1)
+    multiply("A", 1, 0, 2)
     cross_far("B")
-    multiply("A", 2, 4)
-    cross_far("C")
+    multiply("A", 1, 2, 4)
+    relayout("B", 0)
+    multiply("B", 0, 0, 4)
     arrive("B")
-    relayout("B")
-    multiply("B", 0, 4)
-    arrive("C")
-    relayout("C")
-    multiply("C", 0, 4)
+    relayout("B", 1)
+    multiply("B", 1, 0, 4)
 
     lane = lax.broadcasted_iota(jnp.int32, (128, LANE), 1)
 
@@ -264,9 +277,9 @@
 
     fetched(wd, 3)
 
-    def project(name, half, target):
+    def project(name, half, target, pairs):
         first_tile, count, (at, width) = CHUNKS[name]
-        for pair in range(count // 2):
+        for pair in pairs:
             lo = (first_tile + 2 * pair) * LANE
 
             halves = []
@@ -288,14 +301,14 @@
     def ref_of(array, name, index):
         return array.at[index + (slice(None), pl.ds(*CHUNKS[name][2]))]
 
-    def produce_other(name):
-        project(name, 1, other_sum)
-        for split in splits_of(name):
+    def produce_other(name, pair=0):
+        project(name, 1, other_sum, (pair,))
+        for split in (splits_of(name) if name == "C" else (pair,)):
             send(ref_of(other_sum, name, (split,) + place(split)), ref_of(core_got, name, (split,) + place(split)), "core", 0,
-                 ("swap", name), ("swap", name))
-
-    def produce_own(name):
-        project(name, 0, own_sum)
+                 ("swap", name, split), ("swap", name))
+
+    def produce_own(name, pair=0):
+        project(name, 0, own_sum, (pair,))
 
     def group(array, name, index=()):
         some = slice(0, len(splits_of(name)))
@@ -308,9 +321,9 @@
             total = total + array[index + (slice(None), cols)].astype(F32)
         target[0][target[1] + (slice(None), cols)] = total.astype(BF16)
 
-    def reduce_cores(name):
-        received(("swap", name), group(core_got, name))
-        for split in splits_of(name):
+    def reduce_cores(name, splits):
+        for split in splits:
+            received(("swap", name, split), ref_of(core_got, name, (split,) + place(split)))
 
             def slab(z, _, split=split):
                 add(name, (own_sum, (split, z, slice(None), slice(None))), [(core_got, (split, z, slice(None), slice(None)))])
@@ -318,6 +331,12 @@
 
             lax.fori_loop(0, 4, slab, 0)
             axis = ORDERS[split][2]
+            if name == "C":
+                for side, step, array, index in ((FAR, 2, r1, (split,)), (FORWARD, 1, r2, (split, 0)), (BACK, 3, r2, (split, 1))):
+                    key = "far" if side == FAR else "sides"
+                    send(ref_of(own_sum, name, (split,) + place(split, side)), ref_of(array, name, index + plane(split)),
+                         axis, step, (key, name, split), (key, name))
+                continue
             for part, step in ((lower, 1), (upper, 3)):
                 send(ref_of(own_sum, name, (split,) + place(split, FAR, part)), ref_of(r1, name, (split,) + plane(split, part)),
                      axis, step, ("far", step, name, split), ("far", name))
@@ -337,8 +356,11 @@
     def reduce_plane(name):
         for split in splits_of(name):
             received(("sides", name, split), ref_of(r2, name, (split,) + (slice(None),) * 3))
-            add(name, (own_sum, (split,) + place(split, 0)),
-                [(r2, (split, 0) + plane(split)), (r2, (split, 1) + plane(split))])
+            parts = [(r2, (split, 0) + plane(split)), (r2, (split, 1) + plane(split))]
+            if name == "C":
+                received(("far", name, split), ref_of(r1, name, (split,) + plane(split)))
+                parts.append((r1, (split,) + plane(split)))
+            add(name, (own_sum, (split,) + place(split, 0)), parts)
             for step in (1, 3, 2):
                 send(ref_of(own_sum, name, (split,) + place(split, 0, step)), ref_of(r3, name, (split, step, slice(None))),
                      ORDERS[split][1], step, ("row", name, split), ("row", name))
@@ -360,27 +382,29 @@
                 total = total + r4[split, step, :, cols].astype(F32)
             fin[split, :, cols] = total.astype(BF16)
 
+    for split in range(3):
+        produce_other("A", split)
+    for split in range(3):
+        produce_own("A", split)
+        reduce_cores("A", (split,))
+    for split in range(3):
+        produce_other("B", split)
     produce_other("C")
+    for split in range(3):
+        produce_own("B", split)
+        reduce_cores("B", (split,))
     produce_own("C")
-    produce_other("A")
-    reduce_cores("C")
-    produce_own("A")
-    reduce_cores("A")
-    produce_other("B")
-    reduce_far("C")
-    produce_own("B")
-    reduce_cores("B")
-    reduce_plane("C")
     reduce_far("A")
-    reduce_row("C")
+    reduce_cores("C", (0, 1))
     reduce_far("B")
     reduce_plane("A")
-    reduce_last("C")
     reduce_plane("B")
+    reduce_plane("C")
     reduce_row("A")
     reduce_row("B")
-    reduce_last("A")
-    reduce_last("B")
+    reduce_row("C")
+    for name in "ABC":
+        reduce_last(name)
 
     send(fin, fin_got, "core", 0, "last", "last")
     received("last", fin_got)
@@ -399,12 +423,10 @@
                     out[:, col:col + width] = rows.astype(BF16)
     all_sent("entry", got)
     all_sent("first", xs.at[0, :, 0, 0, 1:4])
-    for part, cols in enumerate(parts):
-        all_sent(("second", part), xs.at[0, :, 0, 1:4, :, :, pl.ds(*cols)])
+    all_sent("second", xs.at[0, :, 0, 1:4])
     all_sent("third", xs.at[0, :, 1:3])
     all_sent("passed", xs.at[0, :, 1])
-    all_sent("near", xs.at[1, :, 0])
-    all_sent("cross", xs.at[1, :, 1:4])
+    all_sent("cross", xs.at[1])
     for name in CHUNKS:
         all_sent(("swap", name), group(core_got, name))
         all_sent(("far", name), group(r1, name))

time: 76.1 us -> 70 us (0.920)
  Pallas kernels: 74.4 us -> 68.3 us
    pallas_call x1, Pallas kernels: 74.4 us -> 68.3 us  [on_device(): pl.pallas_call(kernel, out_shape=jax.ShapeDtypeStruct((4, 7168), BF16), i...]
where the time goes in v3:
time: 70 us; the launch traced here: 69.8 us
  Pallas kernels  68.3 us (98%)
  local copies, waits for them, and re-layouts  1.46 us (2%)
    pallas_call x1, Pallas kernels, on_device(): pl.pallas_call(kernel, out_shape=jax.ShapeDtypeStruct((4, 7168), BF16), i...  68.3 us
    unnamed x1, local copies, waits for them, and re-layouts  1.46 us

profile of v3, /device:TPU:1, one launch (start us, length us, event | category | flops | bytes accessed | tf_op | source)
XLA Modules:
  0.0 69.8 jit_solution(14242764585239927930)
XLA Ops:
  0.0 68.3 %shard_map.64 = bf16[4,7168]{1,0:T(4,128)(2,1)} custom-call(bf16[4,7168]{1,0:T(4,128)(2,1)} %tokens.1, s32[4,8]{1,0:T(4,128)} %ids.1, f32[4,8]{1,0:T(4,128)} %weights.1, bf16[2,7168,256]{2,1,0:T(8,128)(2,1)} %w_gate.1, bf16[2,7168,256]{2,1,0:T(8,128)(2,1)} %w_up.1, bf16[2,256,7168]{2,1,0:T(8,128)(2,1)} %w_down.1), custom_call_target="tpu_custom_call" | custom-call | flops 11299999744 | bytes 22100000 | tf_op jit(solution)/shard_map/pallas_call | solution.py:443
  68.4 1.5 %copy.8 = bf16[4,7168]{1,0:T(4,128)(2,1)} copy(bf16[4,7168]{1,0:T(4,128)(2,1)} %shard_map.64) | data formatting | bytes 114688

commit v4 on v3

--- a/solution.py
+++ b/solution.py
@@ -98,7 +98,7 @@
                 for h in range(2):
                     start = pl.multiple_of(side * HALF + h * QUARTER + first * LANE, LANE)
                     fetch(source.at[:, pl.ds(start, count * LANE), :],
-                          wgu[name].at[2 * which:2 * which + 2, pl.ds((half * 2 + h) * count * LANE, count * LANE), :], "ABC".index(name))
+                          wgu[name].at[:, pl.ds((half * 2 + h) * count * LANE, count * LANE), 256 * which:256 * which + 256], "ABC".index(name))
 
     fetch_chunk("A")
 
@@ -208,7 +208,8 @@
                     lhs[name][pl.ds(z * 128, 128), col:col + width] = v[:, h].reshape(128, width).astype(BF16)
                 return 0
 
-            lax.fori_loop(0, 4, rows, 0)
+            for z in range(4):
+                rows(z, 0)
 
     def multiply(name, half, begin, end):
         if half == 0 and begin == 0:
@@ -224,7 +225,8 @@
                 acc[i] += product
             return 0
 
-        lax.fori_loop(begin, end, one, 0)
+        for i in range(begin, end):
+            one(i, 0)
 
     finish_second("C")
     cross_near("C")
@@ -235,25 +237,25 @@
     pass_on("A")
     cross_far("C")
     relayout("C", 0)
-    multiply("C", 0, 0, 4)
+    multiply("C", 0, 0, 2)
     arrive("C")
     relayout("C", 1)
-    multiply("C", 1, 0, 4)
+    multiply("C", 1, 0, 2)
     pass_on("B")
     cross_far("A")
     cross_near("B")
     relayout("A", 0)
-    multiply("A", 0, 0, 4)
+    multiply("A", 0, 0, 2)
     arrive("A")
     relayout("A", 1)
-    multiply("A", 1, 0, 2)
+    multiply("A", 1, 0, 1)
     cross_far("B")
-    multiply("A", 1, 2, 4)
+    multiply("A", 1, 1, 2)
     relayout("B", 0)
-    multiply("B", 0, 0, 4)
+    multiply("B", 0, 0, 2)
     arrive("B")
     relayout("B", 1)
-    multiply("B", 1, 0, 4)
+    multiply("B", 1, 0, 2)
 
     lane = lax.broadcasted_iota(jnp.int32, (128, LANE), 1)
 
@@ -264,16 +266,18 @@
             scale[e, pl.ds(z * 128, 128), :] = jnp.broadcast_to(w, (128, 256))
         return 0
 
-    lax.fori_loop(0, 4, weigh, 0)
+    for z in range(4):
+        weigh(z, 0)
 
     def activate(i, _):
         rows = pl.ds(i * 128, 128)
         for e in range(2):
-            gate = acc[e, rows, :]
-            hid[e, rows, :] = (gate / (1.0 + jnp.exp(-gate)) * acc[2 + e, rows, :]).astype(BF16)
+            gate = acc[e, rows, :256]
+            hid[e, rows, :] = (gate / (1.0 + jnp.exp(-gate)) * acc[e, rows, 256:]).astype(BF16)
         return 0
 
-    lax.fori_loop(0, 4, activate, 0)
+    for i in range(4):
+        activate(i, 0)
 
     fetched(wd, 3)
 
@@ -329,7 +333,8 @@
                 add(name, (own_sum, (split, z, slice(None), slice(None))), [(core_got, (split, z, slice(None), slice(None)))])
                 return 0
 
-            lax.fori_loop(0, 4, slab, 0)
+            for z in range(4):
+                slab(z, 0)
             axis = ORDERS[split][2]
             if name == "C":
                 for side, step, array, index in ((FAR, 2, r1, (split,)), (FORWARD, 1, r2, (split, 0)), (BACK, 3, r2, (split, 1))):
@@ -453,11 +458,11 @@
             pltpu.VMEM((TOKENS, 24 * LANE), BF16),
             pltpu.VMEM((TOKENS, 24 * LANE), BF16),
             pltpu.VMEM((TOKENS, 8 * LANE), BF16),
-            pltpu.VMEM((4, 24 * LANE, 256), BF16),
-            pltpu.VMEM((4, 24 * LANE, 256), BF16),
-            pltpu.VMEM((4, 8 * LANE, 256), BF16),
+            pltpu.VMEM((2, 24 * LANE, 512), BF16),
+            pltpu.VMEM((2, 24 * LANE, 512), BF16),
+            pltpu.VMEM((2, 8 * LANE, 512), BF16),
             pltpu.VMEM((2, 2, 256, HALF), BF16),
-            pltpu.VMEM((4, TOKENS, 256), F32),
+            pltpu.VMEM((2, TOKENS, 512), F32),
             pltpu.VMEM((2, TOKENS, 256), BF16),
             pltpu.VMEM((2, TOKENS, 256), F32),
             pltpu.VMEM(grid3, BF16),

time: 70 us -> 66.6 us (0.951)
  Pallas kernels: 68.3 us -> 64.9 us
    pallas_call x1, Pallas kernels: 68.3 us -> 64.9 us  [on_device(): pl.pallas_call(kernel, out_shape=jax.ShapeDtypeStruct((4, 7168), BF16), i...]
where the time goes in v4:
time: 66.6 us; the launch traced here: 66.4 us
  Pallas kernels  64.9 us (97%)
  local copies, waits for them, and re-layouts  1.46 us (2%)
    pallas_call x1, Pallas kernels, on_device(): pl.pallas_call(kernel, out_shape=jax.ShapeDtypeStruct((4, 7168), BF16), i...  64.9 us
    unnamed x1, local copies, waits for them, and re-layouts  1.46 us

profile of v4, /device:TPU:1, one launch (start us, length us, event | category | flops | bytes accessed | tf_op | source)
XLA Modules:
  0.0 66.4 jit_solution(13282423216333500854)
XLA Ops:
  0.0 64.9 %shard_map.64 = bf16[4,7168]{1,0:T(4,128)(2,1)} custom-call(bf16[4,7168]{1,0:T(4,128)(2,1)} %tokens.1, s32[4,8]{1,0:T(4,128)} %ids.1, f32[4,8]{1,0:T(4,128)} %weights.1, bf16[2,7168,256]{2,1,0:T(8,128)(2,1)} %w_gate.1, bf16[2,7168,256]{2,1,0:T(8,128)(2,1)} %w_up.1, bf16[2,256,7168]{2,1,0:T(8,128)(2,1)} %w_down.1), custom_call_target="tpu_custom_call" | custom-call | flops 11299999744 | bytes 22100000 | tf_op jit(solution)/shard_map/pallas_call | solution.py:448
  64.9 1.5 %copy.8 = bf16[4,7168]{1,0:T(4,128)(2,1)} copy(bf16[4,7168]{1,0:T(4,128)(2,1)} %shard_map.64) | data formatting | bytes 114688

commit v5 on v4

--- a/solution.py
+++ b/solution.py
@@ -241,6 +241,19 @@
     arrive("C")
     relayout("C", 1)
     multiply("C", 1, 0, 2)
+
+    lane = lax.broadcasted_iota(jnp.int32, (128, LANE), 1)
+
+    def weigh(z, _):
+        v = xs[0, 2, z, :, :, :, 512:640].astype(F32).reshape(16, 2, 8, LANE)[:, 0].reshape(128, LANE)
+        for e in range(2):
+            w = jnp.sum(jnp.where(lane % 32 == node * 2 + e, v, 0.0), axis=1, keepdims=True)
+            scale[e, pl.ds(z * 128, 128), :] = jnp.broadcast_to(w, (128, 256))
+        return 0
+
+    for z in range(4):
+        weigh(z, 0)
+
     pass_on("B")
     cross_far("A")
     cross_near("B")
@@ -256,18 +269,6 @@
     arrive("B")
     relayout("B", 1)
     multiply("B", 1, 0, 2)
-
-    lane = lax.broadcasted_iota(jnp.int32, (128, LANE), 1)
-
-    def weigh(z, _):
-        v = xs[0, 2, z, :, :, :, 512:640].astype(F32).reshape(16, 2, 8, LANE)[:, 0].reshape(128, LANE)
-        for e in range(2):
-            w = jnp.sum(jnp.where(lane % 32 == node * 2 + e, v, 0.0), axis=1, keepdims=True)
-            scale[e, pl.ds(z * 128, 128), :] = jnp.broadcast_to(w, (128, 256))
-        return 0
-
-    for z in range(4):
-        weigh(z, 0)
 
     def activate(i, _):
         rows = pl.ds(i * 128, 128)

time: 66.6 us -> 66.6 us (level)
  no operation moved by 1% of the time
where the time goes in v5:
time: 66.6 us; the launch traced here: 66.4 us
  Pallas kernels  64.9 us (97%)
  local copies, waits for them, and re-layouts  1.46 us (2%)
    pallas_call x1, Pallas kernels, on_device(): pl.pallas_call(kernel, out_shape=jax.ShapeDtypeStruct((4, 7168), BF16), i...  64.9 us
    unnamed x1, local copies, waits for them, and re-layouts  1.46 us

profile of v5, /device:TPU:1, one launch (start us, length us, event | category | flops | bytes accessed | tf_op | source)
XLA Modules:
  0.0 66.4 jit_solution(8820561577321811477)
XLA Ops:
  0.0 64.9 %shard_map.64 = bf16[4,7168]{1,0:T(4,128)(2,1)} custom-call(bf16[4,7168]{1,0:T(4,128)(2,1)} %tokens.1, s32[4,8]{1,0:T(4,128)} %ids.1, f32[4,8]{1,0:T(4,128)} %weights.1, bf16[2,7168,256]{2,1,0:T(8,128)(2,1)} %w_gate.1, bf16[2,7168,256]{2,1,0:T(8,128)(2,1)} %w_up.1, bf16[2,256,7168]{2,1,0:T(8,128)(2,1)} %w_down.1), custom_call_target="tpu_custom_call" | custom-call | flops 11299999744 | bytes 22100000 | tf_op jit(solution)/shard_map/pallas_call | solution.py:449
  64.9 1.5 %copy.8 = bf16[4,7168]{1,0:T(4,128)(2,1)} copy(bf16[4,7168]{1,0:T(4,128)(2,1)} %shard_map.64) | data formatting | bytes 114688
